TPU v7x, 512 devices: a whole 4x8x8 slice. The times are simulated.
512 devices in a mesh: tile: 128 (over y, z_hi, x), lev: 4 (over z_lo, core).
Axes of the slice: x: 4, y: 8, z: 8 (z_hi: 4, z_lo: 2; z = z_hi * 2 + z_lo), core: 2. Of those that a mesh axis runs over, the one named last changes fastest.
Arguments:
- tracers: float32 [384, 4, 64, 1024], P('tile', 'lev'), may hold values from -6 to 6
- courant_x: float32 [384, 4, 64, 65], P('tile', 'lev'), may hold values from -0.2 to 0.2
- courant_y: float32 [384, 4, 65, 64], P('tile', 'lev'), may hold values from -0.2 to 0.2
- cell_area: float32 [384, 64, 64], P('tile'), may hold values from 0.5 to 1.5
- neighbor: int32 [384, 4], replicated, may hold values from 0 to 383, as said below
- rotation: int32 [384, 4], replicated, may hold values from 0 to 7, as said below
- weights: float32 [384, 4, 128], P('tile', 'lev'), may hold values from 0.1 to 1
- sounding_column: int32 [384, 128], P('tile'), may hold values from 0 to 4095
- sounding_count: int32 [384], P('tile'), may hold values from 1 to 128
Outputs:
- transported: float32 [384, 4, 64, 1024], P('tile', 'lev')
- column_mean: float32 [384, 16, 128], P('tile')
Inputs may be any that keep to these rules, and one draw needn't show every extreme that they name: `neighbor`: neighbor and rotation describe the edges of a cubed sphere of 6 faces of equal square grids of tiles; tile i lies on index i // 3 of tile. The edge strips that the tiles of one index of tile take from the tiles of another index number at most 3. The rotation codes belong to the same cubed sphere as neighbor.
All inputs are finite; a program needn't handle non-finite values.
Results may differ from a plain program's by a relative error of at most 0.00002.
Values sent between devices are 32-bit elements; how exact they have to be, the bound alone decides.
A program may use at most 64 MiB of HBM per device.

v0:
```python
import jax
import jax.numpy as jnp
from jax import lax
from jax.sharding import PartitionSpec as P

STEPS = 2


def edge_strips(field, members):
    tiles, levels, side, width = field.shape
    west = field[..., :, 0:members]
    east = field[..., :, width - members :]
    south = field[..., 0, :].reshape(tiles, levels, side, members)
    north = field[..., side - 1, :].reshape(tiles, levels, side, members)
    return jnp.stack([west, east, south, north], axis=1)


def surround(field, halos, members):
    tiles, levels, side, width = field.shape
    padded = jnp.pad(field, ((0, 0), (0, 0), (1, 1), (members, members)))
    padded = padded.at[:, :, 1 : side + 1, 0:members].set(halos[:, 0])
    padded = padded.at[:, :, 1 : side + 1, width + members :].set(halos[:, 1])
    padded = padded.at[:, :, 0, members : width + members].set(
        halos[:, 2].reshape(tiles, levels, width)
    )
    padded = padded.at[:, :, side + 1, members : width + members].set(
        halos[:, 3].reshape(tiles, levels, width)
    )
    return padded


def advance(padded, field, courant_x, courant_y, cell_area, members):
    flow_x = jnp.repeat(courant_x, members, axis=3)
    flow_y = jnp.repeat(courant_y, members, axis=3)
    area = jnp.repeat(cell_area, members, axis=2)[:, None]
    flux_x = (
        jnp.maximum(flow_x, 0.0) * padded[:, :, 1:-1, :-members]
        + jnp.minimum(flow_x, 0.0) * padded[:, :, 1:-1, members:]
    )
    flux_y = (
        jnp.maximum(flow_y, 0.0) * padded[:, :, :-1, members:-members]
        + jnp.minimum(flow_y, 0.0) * padded[:, :, 1:, members:-members]
    )
    change = (
        flux_x[..., members:]
        - flux_x[..., :-members]
        + (flux_y[:, :, 1:, :] - flux_y[:, :, :-1, :])
    )
    return field - change / area


def fetch_halos(field, neighbor, rotation, members):
    strips = edge_strips(field, members)
    local_tiles = strips.shape[0]
    myself = lax.axis_index("tile")
    own_partner = lax.dynamic_slice_in_dim(neighbor, myself * local_tiles, local_tiles, 0)
    own_codes = lax.dynamic_slice_in_dim(rotation, myself * local_tiles, local_tiles, 0)
    everyone = lax.all_gather(strips, "tile", axis=0, tiled=True)
    picked = everyone[own_partner, own_codes % 4]
    flipped = (own_codes // 4 == 1)[:, :, None, None, None]
    return jnp.where(flipped, picked[..., ::-1, :], picked)


def body(
    tracers,
    courant_x,
    courant_y,
    cell_area,
    neighbor,
    rotation,
    weights,
    sounding_column,
    sounding_count,
):
    members = tracers.shape[3] // tracers.shape[2]
    field = tracers
    for step in range(STEPS):
        halos = fetch_halos(field, neighbor, rotation, members)
        field = advance(
            surround(field, halos, members), field, courant_x, courant_y, cell_area, members
        )
    tiles, levels, side, width = field.shape
    slots = sounding_column.shape[1]
    flat = field.reshape(tiles, levels, side * side, members)
    index_full = jnp.broadcast_to(
        sounding_column[:, None, :, None], (tiles, levels, slots, members)
    )
    sampled = jnp.take_along_axis(flat, index_full, axis=2)
    weighted = jnp.sum(weights[:, :, :, None] * sampled, axis=1)
    weighted = jnp.transpose(weighted, (0, 2, 1))
    totals = jnp.sum(weights, axis=1)
    live = jnp.arange(slots)[None, :] < sounding_count[:, None]
    weighted, totals = lax.psum((weighted, totals), "lev")
    column_mean = jnp.where(live[:, None, :], weighted / totals[:, None, :], 0.0)
    return (field, column_mean)


def solution(mesh):
    in_specs = (
        P("tile", "lev", None, None),
        P("tile", "lev", None, None),
        P("tile", "lev", None, None),
        P("tile", None, None),
        P(),
        P(),
        P("tile", "lev", None),
        P("tile", None),
        P("tile"),
    )
    out_specs = (P("tile", "lev", None, None), P("tile", None, None))
    return jax.shard_map(body, mesh=mesh, in_specs=in_specs, out_specs=out_specs, check_vma=False)
```

profile of v0, /device:TPU:1, one launch (start us, length us, event | category | flops | bytes accessed | tf_op | source)
XLA Modules:
  0.0 624.2 jit_solution(13814094416153851540)
XLA Ops:
  7.2 1.6 copy.119
  8.8 1.2 slice_reduce_fusion.3
  10.4 0.7 pad_maximum_fusion
  11.2 0.8 fusion.12
  13.3 1.0 copy.118
  14.4 0.7 fusion.18
  15.1 0.8 and_reduce_fusion
  15.9 1.6 maximum_bitcast_fusion
  17.4 183.4 %all-gather.3.cloned.1.call-done = f32[384,4,1,64,16]{3,4,2,1,0:T(8,128)} async-done(((f32[3,4,1,64,16]{3,4,2,1,0:T(8,128)}), f32[384,4,1,64,16]{3,4,2,1,0:T(8,128)}) %all-gather.3.cloned.1.call-update) | async-done | bytes 6291472 | tf_op jit(solution)/shard_map/all_gather | solution.py:58
  200.9 5.2 gather_fusion
  206.3 0.6 fusion.17
  206.9 0.7 copy.113
  207.6 1.7 reshape.524
  209.4 2.4 scatter.26
  211.8 1.4 scatter.29
  213.2 3.7 dynamic-slice_select_fusion.1
  216.8 9.2 %scatter.30 = f32[3,1,66,1056]{2,3,0,1:T(8,128)S(1)} dynamic-update-slice(f32[3,1,66,1056]{2,3,0,1:T(8,128)S(1)} %scatter.29, f32[3,1,1,1024]{2,3,0,1:T(8,128)} %dynamic-slice_select_fusion.1, s32[]{:T(128)} %constant.258.clone.1, s32[]{:T(128)} %constant.258.clone.1, s32[]{:T(128)} %bitcast.8, s32[]{:T(128)} %bitcast.9) | dynamic-update-slice | bytes 24580 | tf_op jit(solution)/shard_map/scatter | solution.py:23
  226.1 0.7 copy.115
  226.8 1.7 reshape.525
  228.5 10.8 %scatter.31 = f32[3,1,66,1056]{2,3,0,1:T(8,128)S(1)} dynamic-update-slice(f32[3,1,66,1056]{2,3,0,1:T(8,128)S(1)} %scatter.30, f32[3,1,1,1024]{2,3,0,1:T(8,128)S(1)} %reshape.525, s32[]{:T(128)} %constant.258.clone.1, s32[]{:T(128)} %constant.258.clone.1, s32[]{:T(128)} %constant.269.clone.1, s32[]{:T(128)} %constant.266.clone.1) | dynamic-update-slice | bytes 24580 | tf_op jit(solution)/shard_map/scatter | solution.py:26
  239.4 0.9 fusion
  240.8 0.9 copy-done.1
  241.7 0.6 fusion.4
  242.3 1.3 slice_reduce_fusion.1
  244.0 0.7 pad_maximum_fusion.1
  245.5 0.6 iota_compare_fusion
  246.6 178.3 %all-gather.5.cloned.1.call-done = f32[384,4,1,64,16]{3,4,0,2,1:T(8,128)} async-done(((f32[3,4,1,64,16]{3,4,0,2,1:T(8,128)}), f32[384,4,1,64,16]{3,4,0,2,1:T(8,128)}) %all-gather.5.cloned.1.call-update) | async-done | bytes 6291472 | tf_op jit(solution)/shard_map/all_gather | solution.py:58
  424.9 5.2 gather_fusion.1
  430.1 0.6 copy.122
  430.7 1.6 rev.7
  432.3 1.0 broadcast_select_fusion
  433.3 0.6 fusion.16
  434.0 0.8 copy.124
  434.8 2.0 reshape.526
  436.8 2.3 scatter.34
  439.2 2.4 scatter.35
  441.5 5.0 dynamic-slice_select_fusion
  446.6 9.2 %scatter.36 = f32[3,1,66,1056]{2,3,0,1:T(8,128)S(1)} dynamic-update-slice(f32[3,1,66,1056]{2,3,0,1:T(8,128)S(1)} %scatter.35, f32[3,1,1,1024]{2,3,0,1:T(8,128)} %dynamic-slice_select_fusion, s32[]{:T(128)} %constant.258.clone.1, s32[]{:T(128)} %constant.258.clone.1, s32[]{:T(128)} %bitcast.8, s32[]{:T(128)} %bitcast.9) | dynamic-update-slice | bytes 24580 | tf_op jit(solution)/shard_map/scatter | solution.py:23
  455.8 0.8 copy.126
  456.6 2.0 reshape.527
  458.7 9.3 %scatter.39 = f32[3,1,66,1056]{2,3,0,1:T(8,128)S(1)} dynamic-update-slice(f32[3,1,66,1056]{2,3,0,1:T(8,128)S(1)} %scatter.36, f32[3,1,1,1024]{2,3,0,1:T(8,128)} %reshape.527, s32[]{:T(128)} %constant.258.clone.1, s32[]{:T(128)} %constant.258.clone.1, s32[]{:T(128)} %constant.269.clone.1, s32[]{:T(128)} %constant.266.clone.1) | dynamic-update-slice | bytes 24580 | tf_op jit(solution)/shard_map/scatter | solution.py:26
  468.0 0.9 fusion.1
  469.8 0.6 fusion.5
  470.9 1.3 copy.130
  472.2 4.1 reshape.499
  476.3 127.0 %gather_fusion.2 = f32[6144]{0:T(1024)S(1)} fusion(f32[3,4096,16]{2,1,0:T(8,128)} %reshape.499, s32[6144]{0:T(1024)S(1)} %reshape.501), kind=kCustom, calls=%fused_computation.2 | custom fusion | bytes 122880 | tf_op jit(solution)/shard_map/jit(take_along_axis)/gather | solution.py:88
  603.8 12.7 %all-reduce.2 = (f32[3,16,128]{1,2,0:T(8,128)S(1)}, f32[3,128]{1,0:T(4,128)S(1)}) all-reduce(f32[3,16,128]{1,2,0:T(8,128)S(1)} %multiply_bitcast_fusion, f32[3,128]{1,0:T(4,128)S(1)} %bitcast.99), channel_id=1, replica_groups=mesh['tile'=128,'lev'=4] {'lev'}, use_global_device_ids=true, to_apply=%region_1.2 | all-reduce | flops 6528 | bytes 52224 | tf_op jit(solution)/shard_map/psum | solution.py:93
  616.6 0.7 copy.131
  (75 shorter events, 6.0 us)
Async XLA Ops:
  7.2 4.0 copy-start.14
  7.2 193.7 %all-gather.3.cloned.1.call-start = ((), (), s32[]{:S(2)}) async-start(), calls=%async_computation | async-start | bytes 12681216 | tf_op jit(solution)/shard_map/all_gather | solution.py:58
  8.8 3.8 copy-start
  11.1 413.7 %all-gather.5.cloned.1.call-start = ((), (), s32[]{:S(2)}) async-start(), calls=%async_computation.1 | async-start | bytes 12681216 | tf_op jit(solution)/shard_map/all_gather | solution.py:58
  12.2 0.9 copy-start.8
  12.2 2.9 copy-start.17
  14.3 226.5 %copy-start.2 = (f32[3,64,64]{1,2,0:T(8,128)}, f32[3,64,64]{1,2,0:T(8,128)S(1)}, u32[]{:S(2)}) copy-start(f32[3,64,64]{1,2,0:T(8,128)S(1)} %copy.118) | copy-start | bytes 147460
  14.4 191.8 %copy-start.13 = (pred[3,4]{0,1:T(4,128)(4,1)}, pred[3,4]{0,1:T(4,128)(4,1)S(1)}, u32[]{:S(2)}) copy-start(pred[3,4]{0,1:T(4,128)(4,1)S(1)} %fusion.9) | copy-start | bytes 40
  216.8 9.2 %copy-start.9 = (f32[3,1,1,64,16]{3,4,0,2,1:T(8,128)S(1)}, f32[3,1,1,64,16]{3,4,0,2,1:T(8,128)}, u32[]{:S(2)}) copy-start(f32[3,1,1,64,16]{3,4,0,2,1:T(8,128)} %get-tuple-element.124) | copy-start | bytes 36868
  239.4 0.9 copy-start.4
  239.4 0.9 copy-start.6
  240.3 1.4 copy-start.1
  242.3 2.4 copy-start.10
  242.3 3.2 copy-start.15
  242.3 3.2 copy-start.18
  244.8 0.6 copy-start.11
  468.0 0.9 copy-start.5
  468.0 0.9 copy-start.7
  468.9 0.9 copy-start.3
  476.3 127.1 %copy-start.12 = (pred[3,128]{1,0:T(4,128)(4,1)S(1)}, pred[3,128]{1,0:T(4,128)(4,1)}, u32[]{:S(2)}) copy-start(pred[3,128]{1,0:T(4,128)(4,1)} %copy-done.11) | copy-start | bytes 1156
  476.3 140.1 %copy-start.16 = (pred[3,128]{1,0:T(4,128)(4,1)S(1)}, pred[3,128]{1,0:T(4,128)(4,1)}, u32[]{:S(2)}) copy-start(pred[3,128]{1,0:T(4,128)(4,1)} %iota_compare_fusion) | copy-start | bytes 1156
Sparse Core Ops, SparseCore 0:
  13.1 187.6 all-gather.2
  244.8 179.9 all-gather.4
where the time goes:
time: 631 us; the launch traced here: 624 us
  waiting for transfers between devices  362 us (57%)
  local copies, waits for them, and re-layouts  216 us (34%)
  other arithmetic  19.3 us (3%)
  between operations  14.6 us (2%)
  blocking collectives  12.7 us (2%)
    all_gather x2, waiting for transfers between devices, fetch_halos(): everyone = lax.all_gather(strips, 'tile', axis=0, tiled=True)  362 us
    gather x4, local copies, waits for them, and re-layouts, body(): sampled = jnp.take_along_axis(flat, index_full, axis=2)  127 us
    scatter x2, local copies, waits for them, and re-layouts, surround(): padded.at[:, :, side + 1, members:width + members]  20.1 us
    scatter x2, local copies, waits for them, and re-layouts, surround(): padded.at[:, :, 0, members:width + members]  18.4 us
    psum x1, blocking collectives, body(): weighted, totals = lax.psum((weighted, totals), 'lev')  12.7 us
  transfers between devices with their start and end apart: 2, of which 2 were waited for; matrix products, arithmetic and copies ran while one was open for 1% of the time, Pallas kernels for 0%

commit v1 on v0

v1 whole, which is shorter than its diff:
```python
import functools

import jax
import jax.numpy as jnp
from jax import lax
from jax.experimental import pallas as pl
from jax.experimental.pallas import tpu as pltpu
from jax.sharding import PartitionSpec as P

MESH = pl.DeviceIdType.MESH
STEPS = 2
TILES_DEV = 3
S = 64
TR = 16
W = S * TR
BLOCKS = W // 128
ROWS = S // 8
NA = 16
NB = 8
SLOTS = 12
CAP_A = 6
CAP_B = 7


def lane_gather(x, index):
    return jnp.take_along_axis(x, index, axis=1, mode="promise_in_bounds")


def iota(shape, axis):
    return lax.broadcasted_iota(jnp.int32, shape, axis)


def plan_kernel(nb_ref, rot_ref, plan_ref, load_ref):
    me = lax.axis_index("tile")
    my_b = me // NA
    code = nb_ref[...] * 8 + rot_ref[...]
    code = jnp.concatenate([code, jnp.zeros((code.shape[0], 124), jnp.int32)], axis=1)
    flat = code.T[0:8]
    sub, lane = iota((8, 128), 0), iota((8, 128), 1)
    edges = []
    for r in range(TILES_DEV):
        at = lane * TILES_DEV + r
        picked = jnp.zeros((8, 128), jnp.int32)
        for block in range(TILES_DEV):
            local = at - 128 * block
            inside = (local >= 0) & (local < 128)
            got = lane_gather(flat[:, 128 * block : 128 * block + 128], jnp.where(inside, local, 0))
            picked = jnp.where(inside, got, picked)
        edges.append(picked[0:4])
    table = jnp.concatenate(edges + [jnp.zeros((4, 128), jnp.int32)], axis=0)
    row = iota((16, 128), 0)
    place = iota((16, 128), 1)
    real = row < SLOTS
    tile = table >> 3
    device = (tile * 21846) >> 16
    slot = (tile - device * TILES_DEV) * 4 + (table & 3)
    flip = (table >> 2) & 1
    dev_a = jnp.where(real, device & (NA - 1), -1)
    dev_b = jnp.where(real, device >> 4, -1)

    def ranks(x):
        total = jnp.zeros((16, 128), jnp.int32)
        for j in range(SLOTS):
            total += jnp.where((row > j) & (x == x[j : j + 1, :]), 1, 0)
        return total

    rank_a, rank_b = ranks(dev_a), ranks(dev_b)
    theirs = []
    for half in range(2):
        part = slice(8 * half, 8 * half + 8)
        got = jnp.zeros((8, 128), jnp.int32)
        for j in range(SLOTS):
            source = jnp.broadcast_to(rank_a[j : j + 1, :], (8, 128))
            got = jnp.where(slot[part] == j, lane_gather(source, device[part]), got)
        theirs.append(got)
    where_a = dev_a * SLOTS + jnp.concatenate(theirs, axis=0)

    def mine(x):
        index = jnp.full((8, 128), me, jnp.int32)
        return jnp.concatenate([lane_gather(x[0:8], index), lane_gather(x[8:16], index)], axis=0)

    my_dev_a, my_dev_b, my_rank_a, my_rank_b = mine(dev_a), mine(dev_b), mine(rank_a), mine(rank_b)
    pack = jnp.zeros((16, 128), jnp.int32)
    forward = jnp.zeros((16, 128), jnp.int32)
    for j in range(SLOTS):
        one = slice(j, j + 1)
        pack += jnp.where((my_dev_a[one] == place) & (my_rank_a[one] == row), j, 0)
        forward += jnp.where((dev_b[one] == my_b) & (rank_b[one] == row), where_a[one], 0)
    plan_ref[0:16, :] = pack
    plan_ref[16:32, :] = forward
    plan_ref[32:48, :] = jnp.where(real, my_dev_b * SLOTS + my_rank_b, 0)
    plan_ref[48:64, :] = mine(flip)
    over_a = jnp.where(real & (dev_a != (place & (NA - 1))) & (rank_a >= CAP_A), 1.0, 0.0)
    over_b = jnp.where(real & (dev_b != (place >> 4)) & (rank_b >= CAP_B), 1.0, 0.0)
    load_ref[0, 0] = jnp.max(jnp.maximum(over_a, over_b))


def main_kernel(
    cap_a,
    cap_b,
    plan_ref,
    count_ref,
    q_ref,
    cx_ref,
    cy_ref,
    area_ref,
    w_ref,
    column_ref,
    out_ref,
    mean_ref,
    field,
    side_w,
    side_e,
    coef,
    strips,
    send_a,
    send_b,
    got_a0,
    got_a1,
    got_b0,
    got_b1,
    level_sum,
    sem_sa,
    sem_ra,
    sem_sb,
    sem_rb,
    sem_sl,
    sem_rl,
):
    me, lev = lax.axis_index("tile"), lax.axis_index("lev")
    my_a, my_b = lax.rem(me, NA), me // NA
    peers_a = [lax.rem(my_a + k, NA) for k in range(NA)]
    peers_b = [lax.rem(my_b + k, NB) for k in range(NB)]
    peers_l = [lax.rem(lev + k, 4) for k in range(4)]

    got_a, got_b = (got_a0, got_a1), (got_b0, got_b1)

    barrier = pltpu.get_barrier_semaphore()
    everyone = [(my_b * NA + a, lev) for a in peers_a[1:]]
    everyone += [(b * NA + my_a, lev) for b in peers_b[1:]]
    everyone += [(me, other) for other in peers_l[1:]]
    for target in everyone:
        pl.semaphore_signal(barrier, inc=1, device_id=target, device_id_type=MESH)

    sub, lane = iota((8, 128), 0), iota((8, 128), 1)
    group, member = lane // TR, lane % TR
    last = 128 - TR

    for t in range(TILES_DEV):
        field[0, t, 8:72, :] = q_ref[t]

    def cut_strips(step):
        for t in range(TILES_DEV):
            for r in range(ROWS):
                rows = slice(8 + 8 * r, 16 + 8 * r)
                for e, start, shift in ((0, 0, 0), (1, W - 128, last)):
                    block = field[step, t, rows, start : start + 128]
                    spread = lane_gather(block, member + shift)
                    line = jnp.sum(jnp.where(group == sub, spread, 0.0), axis=0, keepdims=True)
                    strips[4 * t + e, r : r + 1, :] = line
                block = slice(128 * r, 128 * r + 128)
                strips[4 * t + 2, r : r + 1, :] = field[step, t, 8:9, block]
                strips[4 * t + 3, r : r + 1, :] = field[step, t, 71:72, block]

    def first_hop(step):
        for a in range(NA):
            for k in range(cap_a):
                send_a[step, a, k] = strips[plan_ref[k, a]]
        for k in range(SLOTS):
            got_a[step][my_a * SLOTS + k] = strips[plan_ref[k, my_a]]
        copies = []
        for k in range(1, NA):
            copies.append(
                pltpu.make_async_remote_copy(
                    src_ref=send_a.at[step, peers_a[k], pl.ds(0, cap_a)],
                    dst_ref=got_a[step].at[pl.ds(my_a * SLOTS, cap_a)],
                    send_sem=sem_sa.at[step, k],
                    recv_sem=sem_ra.at[step, k],
                    device_id=(my_b * NA + peers_a[k], lev),
                    device_id_type=MESH,
                )
            )
            copies[-1].start()
        return copies

    def second_hop(step):
        for b in range(NB):
            for k in range(cap_b):
                send_b[step, b, k] = got_a[step][plan_ref[16 + k, b * NA + my_a]]
        for k in range(SLOTS):
            got_b[step][my_b * SLOTS + k] = got_a[step][plan_ref[16 + k, me]]
        copies = []
        for k in range(1, NB):
            copies.append(
                pltpu.make_async_remote_copy(
                    src_ref=send_b.at[step, peers_b[k], pl.ds(0, cap_b)],
                    dst_ref=got_b[step].at[pl.ds(my_b * SLOTS, cap_b)],
                    send_sem=sem_sb.at[step, k],
                    recv_sem=sem_rb.at[step, k],
                    device_id=(peers_b[k] * NA + my_a, lev),
                    device_id_type=MESH,
                )
            )
            copies[-1].start()
        return copies

    def place_halos(step):
        for t in range(TILES_DEV):
            for e in range(4):
                i = 4 * t + e
                strip = got_b[step][plan_ref[32 + i, 0]]
                turned = lane_gather(strip, last - TR * group + member)
                flipped = jnp.full((1, 128), plan_ref[48 + i, 0], jnp.int32) == 1
                for r in range(ROWS):
                    line = jnp.where(flipped, turned[7 - r : 8 - r], strip[r : r + 1])
                    if e < 2:
                        side = side_w if e == 0 else side_e
                        spread = lane_gather(jnp.broadcast_to(line, (8, 128)), TR * sub + member)
                        side[t, 8 * r : 8 * r + 8, :] = spread
                    else:
                        at = 7 if e == 2 else 72
                        field[step, t, at : at + 1, 128 * r : 128 * r + 128] = line

    def coefficients():
        for t in range(TILES_DEV):
            for r in range(ROWS):
                rows = slice(8 * r, 8 * r + 8)
                over = 1.0 / area_ref[t, rows, :]
                cx = cx_ref[t, rows, :]
                west, east = cx[:, 0:S], cx[:, 1 : S + 1]
                south = cy_ref[t, rows, :]
                north = cy_ref[t, 8 * r + 1 : 8 * r + 9, :]
                out = (jnp.maximum(east, 0.0) - jnp.minimum(west, 0.0)) + (
                    jnp.maximum(north, 0.0) - jnp.minimum(south, 0.0)
                )
                compact = (
                    1.0 - out * over,
                    jnp.maximum(west, 0.0) * over,
                    -jnp.minimum(east, 0.0) * over,
                    jnp.maximum(south, 0.0) * over,
                    -jnp.minimum(north, 0.0) * over,
                )
                for n, value in enumerate(compact):
                    wide = jnp.concatenate([value, value], axis=1)
                    for block in range(BLOCKS):
                        coef[n, t, rows, 128 * block : 128 * block + 128] = lane_gather(
                            wide, 8 * block + group
                        )

    def advance(step, write):
        for t in range(TILES_DEV):
            for r in range(ROWS):
                rows = slice(8 * r, 8 * r + 8)
                top = 8 + 8 * r
                cells = [
                    field[step, t, top : top + 8, 128 * b : 128 * b + 128] for b in range(BLOCKS)
                ]
                up = [pltpu.roll(cell, TR, axis=1) for cell in cells]
                down = [pltpu.roll(cell, 128 - TR, axis=1) for cell in cells]
                for b in range(BLOCKS):
                    block = slice(128 * b, 128 * b + 128)
                    before = up[b - 1] if b > 0 else side_w[t, rows, :]
                    after = down[b + 1] if b < BLOCKS - 1 else side_e[t, rows, :]
                    west = jnp.where(lane < TR, before, up[b])
                    east = jnp.where(lane >= last, after, down[b])
                    south = field[step, t, top - 1 : top + 7, block]
                    north = field[step, t, top + 1 : top + 9, block]
                    value = (
                        cells[b] * coef[0, t, rows, block]
                        + (west * coef[1, t, rows, block] + east * coef[2, t, rows, block])
                        + (south * coef[3, t, rows, block] + north * coef[4, t, rows, block])
                    )
                    write(t, rows, block, value)

    def write_next(t, rows, block, value):
        field[1, t, rows.start + 8 : rows.stop + 8, block] = value

    def write_out(t, rows, block, value):
        out_ref[t, rows, block] = value

    cut_strips(0)
    pl.semaphore_wait(barrier, len(everyone))
    sent = []
    for step in range(STEPS):
        if step > 0:
            cut_strips(step)
        copies = first_hop(step)
        sent += copies
        if step == 0:
            coefficients()
        for copy in copies:
            copy.wait_recv()
        copies = second_hop(step)
        sent += copies
        for copy in copies:
            copy.wait_recv()
        place_halos(step)
        advance(step, write_next if step == 0 else write_out)

    mine = level_sum.at[lev]
    for t in range(TILES_DEV):
        column = column_ref[t : t + 1, :]
        weight = w_ref[t : t + 1, :]
        pick = jnp.where(iota((S, 128), 0) == (column >> 6), 1.0, 0.0)
        at = column & (S - 1)
        total = jnp.zeros((TR, 128), jnp.float32)
        for b in range(BLOCKS):
            turned = out_ref[t, :, 128 * b : 128 * b + 128].T
            rows = jnp.dot(
                turned,
                pick,
                preferred_element_type=jnp.float32,
                precision=lax.Precision.HIGHEST,
            )
            for c in range(8):
                total += jnp.where(at == 8 * b + c, rows[TR * c : TR * c + TR], 0.0)
        mine[t, 0:TR, :] = total * weight
        mine[t, TR : TR + 8, :] = jnp.broadcast_to(weight, (8, 128))
    copies = []
    for k in range(1, 4):
        copies.append(
            pltpu.make_async_remote_copy(
                src_ref=level_sum.at[lev],
                dst_ref=level_sum.at[lev],
                send_sem=sem_sl.at[k],
                recv_sem=sem_rl.at[k],
                device_id=(me, peers_l[k]),
                device_id_type=MESH,
            )
        )
        copies[-1].start()
    sent += copies
    for copy in copies:
        copy.wait_recv()
    for t in range(TILES_DEV):
        total = (level_sum[0, t] + level_sum[1, t]) + (level_sum[2, t] + level_sum[3, t])
        live = iota((TR, 128), 1) < count_ref[t]
        mean_ref[t] = jnp.where(live, total[0:TR] / total[TR : TR + 1], 0.0)
    for copy in sent:
        copy.wait_send()


def run_main(cap_a, cap_b, identifier, plan, count, q, cx, cy, area, w, column):
    vmem, smem = pl.BlockSpec(memory_space=pltpu.VMEM), pl.BlockSpec(memory_space=pltpu.SMEM)
    f32 = jnp.float32
    dma = pltpu.SemaphoreType.DMA
    return pl.pallas_call(
        functools.partial(main_kernel, cap_a, cap_b),
        out_shape=(
            jax.ShapeDtypeStruct((TILES_DEV, S, W), f32),
            jax.ShapeDtypeStruct((TILES_DEV, TR, 128), f32),
        ),
        in_specs=[smem] * 2 + [vmem] * 6,
        out_specs=(vmem, vmem),
        scratch_shapes=[
            pltpu.VMEM((2, TILES_DEV, S + 16, W), f32),
            pltpu.VMEM((TILES_DEV, S, 128), f32),
            pltpu.VMEM((TILES_DEV, S, 128), f32),
            pltpu.VMEM((5, TILES_DEV, S, W), f32),
            pltpu.VMEM((SLOTS, 8, 128), f32),
            pltpu.VMEM((2, NA, SLOTS, 8, 128), f32),
            pltpu.VMEM((2, NB, SLOTS, 8, 128), f32),
            pltpu.VMEM((NA * SLOTS, 8, 128), f32),
            pltpu.VMEM((NA * SLOTS, 8, 128), f32),
            pltpu.VMEM((NB * SLOTS, 8, 128), f32),
            pltpu.VMEM((NB * SLOTS, 8, 128), f32),
            pltpu.VMEM((4, TILES_DEV, TR + 8, 128), f32),
            dma((2, NA)),
            dma((2, NA)),
            dma((2, NB)),
            dma((2, NB)),
            dma((4,)),
            dma((4,)),
        ],
        compiler_params=pltpu.CompilerParams(
            collective_id=identifier, has_side_effects=True, vmem_limit_bytes=40 * 2**20
        ),
        name=f"transport_{cap_a}_{cap_b}",
    )(plan, count, q, cx, cy, area, w, column)


def body(
    tracers,
    courant_x,
    courant_y,
    cell_area,
    neighbor,
    rotation,
    weights,
    sounding_column,
    sounding_count,
):
    vmem, smem = pl.BlockSpec(memory_space=pltpu.VMEM), pl.BlockSpec(memory_space=pltpu.SMEM)
    plan, load = pl.pallas_call(
        plan_kernel,
        out_shape=(
            jax.ShapeDtypeStruct((64, 128), jnp.int32),
            jax.ShapeDtypeStruct((1, 1), jnp.float32),
        ),
        in_specs=[vmem, vmem],
        out_specs=(vmem, smem),
        name="plan",
    )(neighbor, rotation)
    operands = (
        plan,
        sounding_count,
        tracers[:, 0],
        courant_x[:, 0],
        courant_y[:, 0],
        cell_area,
        weights[:, 0],
        sounding_column,
    )
    field, mean = lax.cond(
        load[0, 0] > 0.0,
        functools.partial(run_main, SLOTS, SLOTS, 2),
        functools.partial(run_main, CAP_A, CAP_B, 1),
        *operands,
    )
    return field[:, None], mean


def solution(mesh):
    in_specs = (
        P("tile", "lev", None, None),
        P("tile", "lev", None, None),
        P("tile", "lev", None, None),
        P("tile", None, None),
        P(),
        P(),
        P("tile", "lev", None),
        P("tile", None),
        P("tile"),
    )
    out_specs = (P("tile", "lev", None, None), P("tile", None, None))
    return jax.shard_map(body, mesh=mesh, in_specs=in_specs, out_specs=out_specs, check_vma=False)
```

time: 631 us -> 73.1 us (0.12); the launches traced: 624 us -> 72.8 us
  waiting for transfers between devices: 362 us -> 0 us
  local copies, waits for them, and re-layouts: 216 us -> 6.84 us
  Pallas kernels: 0 us -> 64.4 us
  other arithmetic: 19.3 us -> 0 us
  between operations: 14.6 us -> 1.36 us
  blocking collectives: 12.7 us -> 0 us
    all_gather x2 -> x0, waiting for transfers between devices: 362 us -> none  [fetch_halos(): everyone = lax.all_gather(strips, 'tile', axis=0, tiled=True)]
    gather x8 -> x0, local copies, waits for them, and re-layouts: 138 us -> none  [the longest x4 127 us: body(): sampled = jnp.take_along_axis(flat, index_full, axis=2)]
    pallas_call x0 -> x2, Pallas kernels: none -> 64.4 us  [the longest x1 62.5 us: run_main(): pl.pallas_call(functools.partial(main_kernel, cap_a, cap_b), out_shape=(j...]
    scatter x8 -> x0, local copies, waits for them, and re-layouts: 47 us -> none  [the longest x2 20.1 us: surround(): padded.at[:, :, side + 1, members:width + members]]
    psum x1 -> x0, blocking collectives: 12.7 us -> none  [body(): weighted, totals = lax.psum((weighted, totals), 'lev')]
    another operation x6 -> x0, other arithmetic: 10.8 us -> none
    another operation x15 -> x0, local copies, waits for them, and re-layouts: 8.89 us -> none
    slice x8 -> x0, local copies, waits for them, and re-layouts: 6.94 us -> none  [the longest x4 2.81 us: surround(): halos[:, 3].reshape(tiles, levels, width)]
  transfers between devices with their start and end apart: 2 -> 0, of which waited for: 2 -> 0; matrix products, arithmetic and copies ran while one was open for 1% -> 0% of each run, Pallas kernels for 0% -> 0%
where the time goes in v1:
time: 73.1 us; the launch traced here: 72.8 us
  Pallas kernels  64.4 us (88%)
  local copies, waits for them, and re-layouts  6.84 us (9%)
  between operations  1.36 us (2%)
    pallas_call x1, Pallas kernels, run_main(): pl.pallas_call(functools.partial(main_kernel, cap_a, cap_b), out_shape=(j...  62.5 us
    unnamed x18, local copies, waits for them, and re-layouts  6.84 us
    pallas_call x1, Pallas kernels, body(): pl.pallas_call(plan_kernel, out_shape=(jax.ShapeDtypeStruct((64, 128), jn...  1.93 us

profile of v1, /device:TPU:1, one launch (start us, length us, event | category | flops | bytes accessed | tf_op | source)
XLA Modules:
  0.0 72.8 jit_solution(413356244281670767)
XLA Ops:
  0.6 0.0 copy-start.5
  0.6 0.0 copy-start
  0.6 0.7 copy-done.5
  1.3 1.0 %copy.13 = f32[3,1,65,64]{3,2,0,1:T(8,128)S(1)} copy(f32[3,1,65,64]{2,3,1,0:T(8,128)} %param.13) | data formatting | bytes 99840 | tf_op args[2]
  2.3 1.5 %copy.11.nb_ref = s32[384,4]{1,0:T(8,128)} copy(s32[384,4]{0,1:T(4,128)} %param.15) | data formatting | bytes 12288 | tf_op args[4]
  3.8 1.5 %copy.12.rot_ref = s32[384,4]{1,0:T(8,128)} copy(s32[384,4]{0,1:T(4,128)} %param.16) | data formatting | bytes 12288 | tf_op args[5]
  5.3 0.0 copy-start.1
  5.3 0.0 copy-start.2
  5.4 1.9 %plan.1 = (s32[64,128]{1,0:T(8,128)S(1)}, f32[1,1]{1,0:T(1,128)}) custom-call(s32[384,4]{1,0:T(8,128)} %copy.11.nb_ref, s32[384,4]{1,0:T(8,128)} %copy.12.rot_ref), custom_call_target="tpu_custom_call" | custom-call | tf_op jit(solution)/shard_map/plan/pallas_call | solution.py:394
  7.9 0.0 copy-start.3
  8.0 0.0 copy-start.4
  8.0 0.0 copy-done
  8.0 0.0 copy-done.1
  8.0 0.0 copy-done.2
  8.0 0.6 copy-done.3
  8.6 0.0 copy-done.4
  8.6 62.7 %conditional.1 = (f32[3,16,128]{2,1,0:T(8,128)S(1)}, f32[3,1,64,1024]{3,2,1,0:T(8,128)S(1)}) conditional(s32[]{:T(128)} %bitcast.6, (s32[64,128]{1,0:T(8,128)S(1)}, s32[3]{0:T(128)S(1)}, f32[3,64,1024]{2,1,0:T(8,128)S(1)}, f32[3,64,65]{2,1,0:T(8,128)S(1)}, f32[3,65,64]{2,1,0:T(8,128)S(1)}, /*index=5*/f32[3,64,64]{2,1,0:T(8,128)S(1)}, ...), branch_computations={%region_0.0_spmd, %region_1.0_spmd} | conditional | bytes 16 | solution.py:414
  8.6 62.5 %transport_6_7.1 = (f32[3,64,1024]{2,1,0:T(8,128)S(1)}, f32[3,16,128]{2,1,0:T(8,128)S(1)}) custom-call(s32[64,128]{1,0:T(8,128)S(1)} %get-tuple-element.37.plan_ref, s32[3]{0:T(128)S(1)} %get-tuple-element.38.count_ref, f32[3,64,1024]{2,1,0:T(8,128)S(1)} %get-tuple-element.39.q_ref, f32[3,64,65]{2,1,0:T(8,128)S(1)} %get-tuple-element.40.cx_ref, ...), custom_call_target="tpu_custom_call" | custom-call | tf_op jit(solution)/shard_map/cond/branch_0_fun/transport_6_7/pallas_call | solution.py:347
  71.3 0.9 %copy.26 = f32[3,1,64,1024]{3,2,1,0:T(8,128)} copy(f32[3,1,64,1024]{3,2,1,0:T(8,128)S(1)} %get-tuple-element.76) | data formatting | bytes 1572864
  72.2 0.6 copy.27
  (1 shorter events, 0.0 us)
Async XLA Ops:
  0.6 0.7 copy-start.5
  0.6 7.3 %copy-start = (f32[3,1,64,1024]{3,2,1,0:T(8,128)S(1)}, f32[3,1,64,1024]{3,2,1,0:T(8,128)}, u32[]{:S(2)}) copy-start(f32[3,1,64,1024]{3,2,1,0:T(8,128)} %param.11) | copy-start | bytes 2359300
  5.3 2.6 %copy-start.1 = (f32[3,1,64,65]{3,2,1,0:T(8,128)S(1)}, f32[3,1,64,65]{3,2,1,0:T(8,128)}, u32[]{:S(2)}) copy-start(f32[3,1,64,65]{3,2,1,0:T(8,128)} %param.12) | copy-start | bytes 149764
  5.3 2.6 %copy-start.2 = (f32[3,64,64]{2,1,0:T(8,128)S(1)}, f32[3,64,64]{2,1,0:T(8,128)}, u32[]{:S(2)}) copy-start(f32[3,64,64]{2,1,0:T(8,128)} %param.14) | copy-start | bytes 147460
  7.9 0.7 copy-start.3
  8.0 0.7 copy-start.4

commit v2 on v1

--- a/solution.py
+++ b/solution.py
@@ -18,8 +18,10 @@
 NA = 16
 NB = 8
 SLOTS = 12
-CAP_A = 6
-CAP_B = 7
+CAP_A = 3
+CAP_B = 4
+ROUNDS = 3
+INSIDE = (NA + NB) * SLOTS
 
 
 def lane_gather(x, index):
@@ -32,10 +34,9 @@
 
 def plan_kernel(nb_ref, rot_ref, plan_ref, load_ref):
     me = lax.axis_index("tile")
-    my_b = me // NA
+    my_a, my_b = lax.rem(me, NA), me // NA
     code = nb_ref[...] * 8 + rot_ref[...]
-    code = jnp.concatenate([code, jnp.zeros((code.shape[0], 124), jnp.int32)], axis=1)
-    flat = code.T[0:8]
+    flat = jnp.concatenate([code, jnp.zeros(code.shape, jnp.int32)], axis=0)
     sub, lane = iota((8, 128), 0), iota((8, 128), 1)
     edges = []
     for r in range(TILES_DEV):
@@ -57,42 +58,84 @@
     flip = (table >> 2) & 1
     dev_a = jnp.where(real, device & (NA - 1), -1)
     dev_b = jnp.where(real, device >> 4, -1)
-
-    def ranks(x):
-        total = jnp.zeros((16, 128), jnp.int32)
+    use_a = jnp.where(real & (dev_a != (place & (NA - 1))), 1, 0)
+    use_b = jnp.where(real & (dev_b != (place >> 4)), 1, 0)
+    outside = jnp.maximum(use_a, use_b)
+
+    def partner(x):
+        parts = []
+        for half in range(2):
+            part = slice(8 * half, 8 * half + 8)
+            got = jnp.zeros((8, 128), jnp.int32)
+            for j in range(SLOTS):
+                source = jnp.broadcast_to(x[j : j + 1, :], (8, 128))
+                got = jnp.where(slot[part] == j, lane_gather(source, device[part]), got)
+            parts.append(got)
+        return jnp.concatenate(parts, axis=0)
+
+    def count(key, of):
+        every, ahead = jnp.zeros((16, 128), jnp.int32), jnp.zeros((16, 128), jnp.int32)
         for j in range(SLOTS):
-            total += jnp.where((row > j) & (x == x[j : j + 1, :]), 1, 0)
-        return total
-
-    rank_a, rank_b = ranks(dev_a), ranks(dev_b)
-    theirs = []
-    for half in range(2):
-        part = slice(8 * half, 8 * half + 8)
-        got = jnp.zeros((8, 128), jnp.int32)
-        for j in range(SLOTS):
-            source = jnp.broadcast_to(rank_a[j : j + 1, :], (8, 128))
-            got = jnp.where(slot[part] == j, lane_gather(source, device[part]), got)
-        theirs.append(got)
-    where_a = dev_a * SLOTS + jnp.concatenate(theirs, axis=0)
+            one = slice(j, j + 1)
+            same = jnp.where(key == key[one], of[one], 0)
+            every += same
+            ahead += jnp.where(row > j, same, 0)
+        return every, ahead
+
+    own, other = place * SLOTS + row, device * SLOTS + slot
+    mix = jnp.minimum(own, other) * 5 + jnp.maximum(own, other) * 3
+    by_a = jnp.where(own < other, 1, 0) ^ ((mix >> 2) & 1)
+    for turn in range(ROUNDS):
+        all_a, ahead_a = count(dev_a, by_a * use_a)
+        all_b, ahead_b = count(dev_b, (1 - by_a) * use_b)
+        first = by_a == 1
+        late = jnp.where(
+            first, jnp.where(ahead_a >= CAP_A, use_a, 0), jnp.where(ahead_b >= CAP_B, use_b, 0)
+        )
+        over_a, more_a = jnp.maximum(all_a - CAP_A, 0), jnp.maximum(all_a + 1 - CAP_A, 0)
+        over_b, more_b = jnp.maximum(all_b - CAP_B, 0), jnp.maximum(all_b + 1 - CAP_B, 0)
+        gain = jnp.where(
+            first, over_a * use_a - more_b * use_b, over_b * use_b - more_a * use_a
+        )
+        theirs = partner((gain + 64) * 2 + late)
+        wanted = late | (theirs & 1)
+        better = (gain + (theirs >> 1) - 64) > 0
+        now = ((mix >> 1) + turn) & 1
+        by_a = jnp.where(better & (now == 0), by_a ^ (wanted & outside), by_a)
+
+    go_a, go_b = by_a * outside, (1 - by_a) * outside
+    rank_a, rank_b = count(dev_a, go_a)[1], count(dev_b, go_b)[1]
+    theirs = partner(rank_a * 16 + rank_b)
+    at_a = dev_a * SLOTS + (theirs >> 4)
+    at_b = dev_b * SLOTS + (theirs & 15)
 
     def mine(x):
         index = jnp.full((8, 128), me, jnp.int32)
         return jnp.concatenate([lane_gather(x[0:8], index), lane_gather(x[8:16], index)], axis=0)
 
-    my_dev_a, my_dev_b, my_rank_a, my_rank_b = mine(dev_a), mine(dev_b), mine(rank_a), mine(rank_b)
-    pack = jnp.zeros((16, 128), jnp.int32)
-    forward = jnp.zeros((16, 128), jnp.int32)
+    key_a = jnp.where(go_a == 1, dev_a * 16 + rank_a, -1)
+    key_b = jnp.where(go_b == 1, dev_b * 16 + rank_b, -1)
+    my_key_a, my_key_b = mine(key_a), mine(key_b)
+    pack_a, pack_b, forward_a, forward_b = (jnp.zeros((16, 128), jnp.int32) for _ in range(4))
     for j in range(SLOTS):
         one = slice(j, j + 1)
-        pack += jnp.where((my_dev_a[one] == place) & (my_rank_a[one] == row), j, 0)
-        forward += jnp.where((dev_b[one] == my_b) & (rank_b[one] == row), where_a[one], 0)
-    plan_ref[0:16, :] = pack
-    plan_ref[16:32, :] = forward
-    plan_ref[32:48, :] = jnp.where(real, my_dev_b * SLOTS + my_rank_b, 0)
-    plan_ref[48:64, :] = mine(flip)
-    over_a = jnp.where(real & (dev_a != (place & (NA - 1))) & (rank_a >= CAP_A), 1.0, 0.0)
-    over_b = jnp.where(real & (dev_b != (place >> 4)) & (rank_b >= CAP_B), 1.0, 0.0)
-    load_ref[0, 0] = jnp.max(jnp.maximum(over_a, over_b))
+        pack_a += jnp.where(my_key_a[one] == place * 16 + row, j, 0)
+        pack_b += jnp.where(my_key_b[one] == place * 16 + row, j, 0)
+        forward_a += jnp.where(key_a[one] == my_a * 16 + row, at_b[one], 0)
+        forward_b += jnp.where(key_b[one] == my_b * 16 + row, at_a[one], 0)
+    take = jnp.where(
+        go_a == 1,
+        NB * SLOTS + dev_a * SLOTS + rank_a,
+        jnp.where(go_b == 1, dev_b * SLOTS + rank_b, (NA + NB) * SLOTS + slot),
+    )
+    plan_ref[0:16, :] = pack_a
+    plan_ref[16:32, :] = pack_b
+    plan_ref[32:48, :] = forward_a
+    plan_ref[48:64, :] = forward_b
+    plan_ref[64:80, :] = mine(jnp.where(real, take * 2 + flip, 0))
+    full_a = jnp.where((go_a * use_a == 1) & (rank_a >= CAP_A), 1.0, 0.0)
+    full_b = jnp.where((go_b * use_b == 1) & (rank_b >= CAP_B), 1.0, 0.0)
+    load_ref[0, 0] = jnp.max(jnp.maximum(full_a, full_b))
 
 
 def main_kernel(
@@ -119,6 +162,8 @@
     got_a1,
     got_b0,
     got_b1,
+    arrived0,
+    arrived1,
     level_sum,
     sem_sa,
     sem_ra,
@@ -129,15 +174,16 @@
 ):
     me, lev = lax.axis_index("tile"), lax.axis_index("lev")
     my_a, my_b = lax.rem(me, NA), me // NA
-    peers_a = [lax.rem(my_a + k, NA) for k in range(NA)]
-    peers_b = [lax.rem(my_b + k, NB) for k in range(NB)]
+    my_z, my_x = my_a // 4, lax.rem(my_a, 4)
+    shifts = sorted(range(1, NA), key=lambda k: -2 * min(k // 4, 4 - k // 4) - min(k % 4, 4 - k % 4))
+    peers_a = {k: lax.rem(my_z + k // 4, 4) * 4 + lax.rem(my_x + k % 4, 4) for k in shifts}
+    peers_b = {k: lax.rem(my_b + k, NB) for k in sorted(range(1, NB), key=lambda k: -min(k, NB - k))}
     peers_l = [lax.rem(lev + k, 4) for k in range(4)]
-
-    got_a, got_b = (got_a0, got_a1), (got_b0, got_b1)
+    got_a, got_b, arrived = (got_a0, got_a1), (got_b0, got_b1), (arrived0, arrived1)
 
     barrier = pltpu.get_barrier_semaphore()
-    everyone = [(my_b * NA + a, lev) for a in peers_a[1:]]
-    everyone += [(b * NA + my_a, lev) for b in peers_b[1:]]
+    everyone = [(my_b * NA + a, lev) for a in peers_a.values()]
+    everyone += [(b * NA + my_a, lev) for b in peers_b.values()]
     everyone += [(me, other) for other in peers_l[1:]]
     for target in everyone:
         pl.semaphore_signal(barrier, inc=1, device_id=target, device_id_type=MESH)
@@ -162,55 +208,93 @@
                 strips[4 * t + 2, r : r + 1, :] = field[step, t, 8:9, block]
                 strips[4 * t + 3, r : r + 1, :] = field[step, t, 71:72, block]
 
-    def first_hop(step):
-        for a in range(NA):
-            for k in range(cap_a):
-                send_a[step, a, k] = strips[plan_ref[k, a]]
+    def move(ref, index, cap, own, source, at, to, base):
+        for other in range(index[1]):
+            lane = index[2](other)
+            for k in range(cap):
+                ref[other, k] = source[plan_ref[index[0] + k, lane]]
         for k in range(SLOTS):
-            got_a[step][my_a * SLOTS + k] = strips[plan_ref[k, my_a]]
+            to[base + own * SLOTS + k] = source[plan_ref[index[0] + k, at]]
+
+    def send_in_plane(hop, step, dst, base):
         copies = []
-        for k in range(1, NA):
+        for k, peer in peers_a.items():
             copies.append(
                 pltpu.make_async_remote_copy(
-                    src_ref=send_a.at[step, peers_a[k], pl.ds(0, cap_a)],
-                    dst_ref=got_a[step].at[pl.ds(my_a * SLOTS, cap_a)],
-                    send_sem=sem_sa.at[step, k],
-                    recv_sem=sem_ra.at[step, k],
-                    device_id=(my_b * NA + peers_a[k], lev),
+                    src_ref=send_a.at[hop, step, peer, pl.ds(0, cap_a)],
+                    dst_ref=dst.at[pl.ds(base + my_a * SLOTS, cap_a)],
+                    send_sem=sem_sa.at[hop, step, k],
+                    recv_sem=sem_ra.at[hop, step, k],
+                    device_id=(my_b * NA + peer, lev),
                     device_id_type=MESH,
                 )
             )
             copies[-1].start()
         return copies
 
-    def second_hop(step):
-        for b in range(NB):
-            for k in range(cap_b):
-                send_b[step, b, k] = got_a[step][plan_ref[16 + k, b * NA + my_a]]
-        for k in range(SLOTS):
-            got_b[step][my_b * SLOTS + k] = got_a[step][plan_ref[16 + k, me]]
+    def send_along_y(hop, step, dst, base):
         copies = []
-        for k in range(1, NB):
+        for k, peer in peers_b.items():
             copies.append(
                 pltpu.make_async_remote_copy(
-                    src_ref=send_b.at[step, peers_b[k], pl.ds(0, cap_b)],
-                    dst_ref=got_b[step].at[pl.ds(my_b * SLOTS, cap_b)],
-                    send_sem=sem_sb.at[step, k],
-                    recv_sem=sem_rb.at[step, k],
-                    device_id=(peers_b[k] * NA + my_a, lev),
+                    src_ref=send_b.at[hop, step, peer, pl.ds(0, cap_b)],
+                    dst_ref=dst.at[pl.ds(base + my_b * SLOTS, cap_b)],
+                    send_sem=sem_sb.at[hop, step, k],
+                    recv_sem=sem_rb.at[hop, step, k],
+                    device_id=(peer * NA + my_a, lev),
                     device_id_type=MESH,
                 )
             )
             copies[-1].start()
         return copies
 
+    def exchange(step, meanwhile):
+        here = arrived[step]
+        move(send_a.at[0, step], (0, NA, lambda a: a), cap_a, my_a, strips, my_a, got_a[step], 0)
+        one_a = send_in_plane(0, step, got_a[step], 0)
+        move(send_b.at[0, step], (16, NB, lambda b: b), cap_b, my_b, strips, my_b, got_b[step], 0)
+        one_b = send_along_y(0, step, got_b[step], 0)
+        for k in range(SLOTS):
+            here[INSIDE + k] = strips[k]
+        meanwhile()
+        for copy in one_b:
+            copy.wait_recv()
+        move(
+            send_a.at[1, step],
+            (32, NA, lambda a: my_b * NA + a),
+            cap_a,
+            my_a,
+            got_b[step],
+            me,
+            here,
+            NB * SLOTS,
+        )
+        two_a = send_in_plane(1, step, here, NB * SLOTS)
+        for copy in one_a:
+            copy.wait_recv()
+        move(
+            send_b.at[1, step],
+            (48, NB, lambda b: b * NA + my_a),
+            cap_b,
+            my_b,
+            got_a[step],
+            me,
+            here,
+            0,
+        )
+        two_b = send_along_y(1, step, here, 0)
+        for copy in two_b + two_a:
+            copy.wait_recv()
+        return one_a + one_b + two_a + two_b
+
     def place_halos(step):
         for t in range(TILES_DEV):
             for e in range(4):
                 i = 4 * t + e
-                strip = got_b[step][plan_ref[32 + i, 0]]
+                taken = plan_ref[64 + i, 0]
+                strip = arrived[step][taken >> 1]
                 turned = lane_gather(strip, last - TR * group + member)
-                flipped = jnp.full((1, 128), plan_ref[48 + i, 0], jnp.int32) == 1
+                flipped = jnp.full((1, 128), taken & 1, jnp.int32) == 1
                 for r in range(ROWS):
                     line = jnp.where(flipped, turned[7 - r : 8 - r], strip[r : r + 1])
                     if e < 2:
@@ -222,30 +306,31 @@
                         field[step, t, at : at + 1, 128 * r : 128 * r + 128] = line
 
     def coefficients():
+        at, to = iota((4 * S, W), 0), iota((4 * S, W), 1)
+        repeat = jnp.where(((at & (S - 1)) == (to >> 4)) & (at < 3 * S), 1.0, 0.0)
+        repeat = repeat.astype(jnp.bfloat16)
         for t in range(TILES_DEV):
-            for r in range(ROWS):
-                rows = slice(8 * r, 8 * r + 8)
-                over = 1.0 / area_ref[t, rows, :]
-                cx = cx_ref[t, rows, :]
-                west, east = cx[:, 0:S], cx[:, 1 : S + 1]
-                south = cy_ref[t, rows, :]
-                north = cy_ref[t, 8 * r + 1 : 8 * r + 9, :]
-                out = (jnp.maximum(east, 0.0) - jnp.minimum(west, 0.0)) + (
-                    jnp.maximum(north, 0.0) - jnp.minimum(south, 0.0)
-                )
-                compact = (
-                    1.0 - out * over,
-                    jnp.maximum(west, 0.0) * over,
-                    -jnp.minimum(east, 0.0) * over,
-                    jnp.maximum(south, 0.0) * over,
-                    -jnp.minimum(north, 0.0) * over,
-                )
-                for n, value in enumerate(compact):
-                    wide = jnp.concatenate([value, value], axis=1)
-                    for block in range(BLOCKS):
-                        coef[n, t, rows, 128 * block : 128 * block + 128] = lane_gather(
-                            wide, 8 * block + group
-                        )
+            over = 1.0 / area_ref[t]
+            cx, cy = cx_ref[t], cy_ref[t].T
+            west, east = cx[:, 0:S], cx[:, 1 : S + 1]
+            south, north = cy[0:S], cy[1 : S + 1]
+            out = (jnp.maximum(east, 0.0) - jnp.minimum(west, 0.0)) + (
+                jnp.maximum(north, 0.0) - jnp.minimum(south, 0.0)
+            )
+            compact = (
+                1.0 - out * over,
+                jnp.maximum(west, 0.0) * over,
+                -jnp.minimum(east, 0.0) * over,
+                jnp.maximum(south, 0.0) * over,
+                -jnp.minimum(north, 0.0) * over,
+            )
+            for n, value in enumerate(compact):
+                high = value.astype(jnp.bfloat16).astype(jnp.float32)
+                rest = value - high
+                middle = rest.astype(jnp.bfloat16).astype(jnp.float32)
+                parts = [high, middle, rest - middle, jnp.zeros((S, S), jnp.float32)]
+                parts = jnp.concatenate(parts, axis=1).astype(jnp.bfloat16)
+                coef[n, t] = jnp.dot(parts, repeat, preferred_element_type=jnp.float32)
 
     def advance(step, write):
         for t in range(TILES_DEV):
@@ -284,23 +369,14 @@
     for step in range(STEPS):
         if step > 0:
             cut_strips(step)
-        copies = first_hop(step)
-        sent += copies
-        if step == 0:
-            coefficients()
-        for copy in copies:
-            copy.wait_recv()
-        copies = second_hop(step)
-        sent += copies
-        for copy in copies:
-            copy.wait_recv()
+        sent += exchange(step, coefficients if step == 0 else lambda: None)
         place_halos(step)
         advance(step, write_next if step == 0 else write_out)
 
     mine = level_sum.at[lev]
     for t in range(TILES_DEV):
         column = column_ref[t : t + 1, :]
-        weight = w_ref[t : t + 1, :]
+        weight = w_ref[t]
         pick = jnp.where(iota((S, 128), 0) == (column >> 6), 1.0, 0.0)
         at = column & (S - 1)
         total = jnp.zeros((TR, 128), jnp.float32)
@@ -358,17 +434,19 @@
             pltpu.VMEM((TILES_DEV, S, 128), f32),
             pltpu.VMEM((5, TILES_DEV, S, W), f32),
             pltpu.VMEM((SLOTS, 8, 128), f32),
-            pltpu.VMEM((2, NA, SLOTS, 8, 128), f32),
-            pltpu.VMEM((2, NB, SLOTS, 8, 128), f32),
+            pltpu.VMEM((2, 2, NA, SLOTS, 8, 128), f32),
+            pltpu.VMEM((2, 2, NB, SLOTS, 8, 128), f32),
             pltpu.VMEM((NA * SLOTS, 8, 128), f32),
             pltpu.VMEM((NA * SLOTS, 8, 128), f32),
             pltpu.VMEM((NB * SLOTS, 8, 128), f32),
             pltpu.VMEM((NB * SLOTS, 8, 128), f32),
+            pltpu.VMEM((INSIDE + SLOTS, 8, 128), f32),
+            pltpu.VMEM((INSIDE + SLOTS, 8, 128), f32),
             pltpu.VMEM((4, TILES_DEV, TR + 8, 128), f32),
-            dma((2, NA)),
-            dma((2, NA)),
-            dma((2, NB)),
-            dma((2, NB)),
+            dma((2, 2, NA)),
+            dma((2, 2, NA)),
+            dma((2, 2, NB)),
+            dma((2, 2, NB)),
             dma((4,)),
             dma((4,)),
         ],
@@ -394,21 +472,21 @@
     plan, load = pl.pallas_call(
         plan_kernel,
         out_shape=(
-            jax.ShapeDtypeStruct((64, 128), jnp.int32),
+            jax.ShapeDtypeStruct((80, 128), jnp.int32),
             jax.ShapeDtypeStruct((1, 1), jnp.float32),
         ),
         in_specs=[vmem, vmem],
         out_specs=(vmem, smem),
         name="plan",
-    )(neighbor, rotation)
+    )(neighbor.T, rotation.T)
     operands = (
         plan,
         sounding_count,
         tracers[:, 0],
         courant_x[:, 0],
-        courant_y[:, 0],
+        jnp.swapaxes(courant_y[:, 0], 1, 2),
         cell_area,
-        weights[:, 0],
+        weights,
         sounding_column,
     )
     field, mean = lax.cond(

time: 73.1 us -> 57.1 us (0.78)
  Pallas kernels: 64.4 us -> 53.2 us
  local copies, waits for them, and re-layouts: 6.84 us -> 2.18 us
    pallas_call x1, Pallas kernels: 62.5 us -> 51.3 us  [run_main(): pl.pallas_call(functools.partial(main_kernel, cap_a, cap_b), out_shape=(j...]
    unnamed x18 -> x8, local copies, waits for them, and re-layouts: 6.84 us -> 2.18 us
where the time goes in v2:
time: 57.1 us; the launch traced here: 56.9 us
  Pallas kernels  53.2 us (93%)
  local copies, waits for them, and re-layouts  2.18 us (4%)
  between operations  1.32 us (2%)
    pallas_call x1, Pallas kernels, run_main(): pl.pallas_call(functools.partial(main_kernel, cap_a, cap_b), out_shape=(j...  51.3 us
    unnamed x8, local copies, waits for them, and re-layouts  2.18 us
    pallas_call x1, Pallas kernels, body(): pl.pallas_call(plan_kernel, out_shape=(jax.ShapeDtypeStruct((80, 128), jn...  1.9 us

profile of v2, /device:TPU:1, one launch (start us, length us, event | category | flops | bytes accessed | tf_op | source)
XLA Modules:
  0.0 56.9 jit_solution(4835784751567026360)
XLA Ops:
  0.6 1.9 %plan.1 = (s32[80,128]{1,0:T(8,128)S(1)}, f32[1,1]{1,0:T(1,128)}) custom-call(s32[4,384]{1,0:T(4,128)} %bitcast.28, s32[4,384]{1,0:T(4,128)} %bitcast.29), custom_call_target="tpu_custom_call" | custom-call | tf_op jit(solution)/shard_map/plan/pallas_call | solution.py:472
  3.2 0.0 copy-start.2
  3.2 0.0 copy-start
  3.2 0.0 copy-start.1
  3.2 0.6 %copy-done.2 = s32[3]{0:T(128)S(1)} copy-done((s32[3]{0:T(128)S(1)}, s32[3]{0:T(128)}, u32[]{:S(2)}) %copy-start.2) | copy-done | bytes 36
  3.8 0.0 copy-done
  3.9 0.0 copy-done.1
  3.9 51.5 %conditional.1 = (f32[3,16,128]{2,1,0:T(8,128)S(1)}, f32[3,1,64,1024]{3,2,1,0:T(8,128)S(1)}) conditional(s32[]{:T(128)} %bitcast.16, (f32[3,1,64,1024]{3,2,1,0:T(8,128)}, f32[3,1,64,65]{3,2,1,0:T(8,128)}, s32[80,128]{1,0:T(8,128)S(1)}, s32[3]{0:T(128)S(1)}, f32[3,64,65]{2,1,0:T(8,128)}, /*index=5*/f32[3,64,64]{2,1,0:T(8,128)}, ...), branch_computations={%region_0.0_spmd, %region_1.0_spmd} | conditional | bytes 16 | solution.py:492
  3.9 51.3 %transport_3_4.1 = (f32[3,64,1024]{2,1,0:T(8,128)S(1)}, f32[3,16,128]{2,1,0:T(8,128)S(1)}) custom-call(s32[80,128]{1,0:T(8,128)S(1)} %get-tuple-element.41.plan_ref, s32[3]{0:T(128)S(1)} %get-tuple-element.42.count_ref, f32[3,64,1024]{2,1,0:T(8,128)} %bitcast.20, f32[3,64,65]{2,1,0:T(8,128)} %bitcast.24, f32[3,64,65]{2,1,0:T(8,128)} %get-tuple-element.45.cy_ref, ...), custom_call_target="tpu_custom_call" | custom-call | tf_op jit(solution)/shard_map/cond/branch_0_fun/transport_3_4/pallas_call | solution.py:423
  55.4 0.9 %copy.24 = f32[3,1,64,1024]{3,2,1,0:T(8,128)} copy(f32[3,1,64,1024]{3,2,1,0:T(8,128)S(1)} %get-tuple-element.96) | data formatting | bytes 1572864
  56.3 0.6 %copy.25 = f32[3,16,128]{2,1,0:T(8,128)} copy(f32[3,16,128]{2,1,0:T(8,128)S(1)} %get-tuple-element.97) | data formatting | bytes 49152
Async XLA Ops:
  3.2 0.7 %copy-start.2 = (s32[3]{0:T(128)S(1)}, s32[3]{0:T(128)}, u32[]{:S(2)}) copy-start(s32[3]{0:T(128)} %param.19) | copy-start | bytes 40
  3.2 0.7 %copy-start = (s32[3,128]{1,0:T(4,128)S(1)}, s32[3,128]{1,0:T(4,128)}, u32[]{:S(2)}) copy-start(s32[3,128]{1,0:T(4,128)} %param.18) | copy-start | bytes 4612
  3.2 0.7 %copy-start.1 = (f32[3,1,128]{2,1,0:T(1,128)S(1)}, f32[3,1,128]{2,1,0:T(1,128)}, u32[]{:S(2)}) copy-start(f32[3,1,128]{2,1,0:T(1,128)} %param.17) | copy-start | bytes 4612

commit v3 on v2

--- a/solution.py
+++ b/solution.py
@@ -18,9 +18,9 @@
 NA = 16
 NB = 8
 SLOTS = 12
-CAP_A = 3
+CAP_A = 2
 CAP_B = 4
-ROUNDS = 3
+ROUNDS = 14
 INSIDE = (NA + NB) * SLOTS
 
 
@@ -89,8 +89,9 @@
         all_a, ahead_a = count(dev_a, by_a * use_a)
         all_b, ahead_b = count(dev_b, (1 - by_a) * use_b)
         first = by_a == 1
+        high_a, high_b = (ahead_a + 1, ahead_b + 1) if turn < 2 else (all_a, all_b)
         late = jnp.where(
-            first, jnp.where(ahead_a >= CAP_A, use_a, 0), jnp.where(ahead_b >= CAP_B, use_b, 0)
+            first, jnp.where(high_a > CAP_A, use_a, 0), jnp.where(high_b > CAP_B, use_b, 0)
         )
         over_a, more_a = jnp.maximum(all_a - CAP_A, 0), jnp.maximum(all_a + 1 - CAP_A, 0)
         over_b, more_b = jnp.maximum(all_b - CAP_B, 0), jnp.maximum(all_b + 1 - CAP_B, 0)
@@ -99,9 +100,10 @@
         )
         theirs = partner((gain + 64) * 2 + late)
         wanted = late | (theirs & 1)
-        better = (gain + (theirs >> 1) - 64) > 0
-        now = ((mix >> 1) + turn) & 1
-        by_a = jnp.where(better & (now == 0), by_a ^ (wanted & outside), by_a)
+        least = 1 if turn < 2 else 0
+        better = gain + (theirs >> 1) - 64 >= least
+        now = (mix >> 1) + turn if turn < 2 else (mix * 7919 + turn * 104729) >> 5
+        by_a = jnp.where(better & (now & 1 == 0), by_a ^ (wanted & outside), by_a)
 
     go_a, go_b = by_a * outside, (1 - by_a) * outside
     rank_a, rank_b = count(dev_a, go_a)[1], count(dev_b, go_b)[1]
@@ -152,8 +154,6 @@
     out_ref,
     mean_ref,
     field,
-    side_w,
-    side_e,
     coef,
     strips,
     send_a,
@@ -193,6 +193,9 @@
     last = 128 - TR
 
     for t in range(TILES_DEV):
+        for step in range(STEPS):
+            for at in (7, 72):
+                field[step, t, at : at + 1, :] = jnp.zeros((1, W), jnp.float32)
         field[0, t, 8:72, :] = q_ref[t]
 
     def cut_strips(step):
@@ -208,86 +211,82 @@
                 strips[4 * t + 2, r : r + 1, :] = field[step, t, 8:9, block]
                 strips[4 * t + 3, r : r + 1, :] = field[step, t, 71:72, block]
 
-    def move(ref, index, cap, own, source, at, to, base):
-        for other in range(index[1]):
-            lane = index[2](other)
-            for k in range(cap):
-                ref[other, k] = source[plan_ref[index[0] + k, lane]]
-        for k in range(SLOTS):
-            to[base + own * SLOTS + k] = source[plan_ref[index[0] + k, at]]
-
-    def send_in_plane(hop, step, dst, base):
+    def send(peers, cap, lane_of, first, source, ref, dst, base, sems, target):
         copies = []
-        for k, peer in peers_a.items():
+        for k, peer in peers.items():
+            for n in range(cap):
+                ref[peer, n] = source[plan_ref[first + n, lane_of(peer)]]
             copies.append(
                 pltpu.make_async_remote_copy(
-                    src_ref=send_a.at[hop, step, peer, pl.ds(0, cap_a)],
-                    dst_ref=dst.at[pl.ds(base + my_a * SLOTS, cap_a)],
-                    send_sem=sem_sa.at[hop, step, k],
-                    recv_sem=sem_ra.at[hop, step, k],
-                    device_id=(my_b * NA + peer, lev),
+                    src_ref=ref.at[peer, pl.ds(0, cap)],
+                    dst_ref=dst.at[pl.ds(base, cap)],
+                    send_sem=sems[0].at[k],
+                    recv_sem=sems[1].at[k],
+                    device_id=target(peer),
                     device_id_type=MESH,
                 )
             )
-            copies[-1].start()
+            if len(copies) > 1:
+                copies[-2].start()
+        copies[-1].start()
         return copies
 
-    def send_along_y(hop, step, dst, base):
-        copies = []
-        for k, peer in peers_b.items():
-            copies.append(
-                pltpu.make_async_remote_copy(
-                    src_ref=send_b.at[hop, step, peer, pl.ds(0, cap_b)],
-                    dst_ref=dst.at[pl.ds(base + my_b * SLOTS, cap_b)],
-                    send_sem=sem_sb.at[hop, step, k],
-                    recv_sem=sem_rb.at[hop, step, k],
-                    device_id=(peer * NA + my_a, lev),
-                    device_id_type=MESH,
-                )
-            )
-            copies[-1].start()
-        return copies
+    def send_in_plane(hop, step, first, lane_of, source, dst, base):
+        return send(
+            peers_a,
+            cap_a,
+            lane_of,
+            first,
+            source,
+            send_a.at[hop, step],
+            dst,
+            base + my_a * SLOTS,
+            (sem_sa.at[hop, step], sem_ra.at[hop, step]),
+            lambda peer: (my_b * NA + peer, lev),
+        )
+
+    def send_along_y(hop, step, first, lane_of, source, dst, base):
+        return send(
+            peers_b,
+            cap_b,
+            lane_of,
+            first,
+            source,
+            send_b.at[hop, step],
+            dst,
+            base + my_b * SLOTS,
+            (sem_sb.at[hop, step], sem_rb.at[hop, step]),
+            lambda peer: (peer * NA + my_a, lev),
+        )
+
+    def keep(first, lane, source, to, base):
+        for n in range(SLOTS):
+            to[base + n] = source[plan_ref[first + n, lane]]
 
     def exchange(step, meanwhile):
         here = arrived[step]
-        move(send_a.at[0, step], (0, NA, lambda a: a), cap_a, my_a, strips, my_a, got_a[step], 0)
-        one_a = send_in_plane(0, step, got_a[step], 0)
-        move(send_b.at[0, step], (16, NB, lambda b: b), cap_b, my_b, strips, my_b, got_b[step], 0)
-        one_b = send_along_y(0, step, got_b[step], 0)
+        one_a = send_in_plane(0, step, 0, lambda a: a, strips, got_a[step], 0)
+        one_b = send_along_y(0, step, 16, lambda b: b, strips, got_b[step], 0)
+        keep(0, my_a, strips, got_a[step], my_a * SLOTS)
+        keep(16, my_b, strips, got_b[step], my_b * SLOTS)
         for k in range(SLOTS):
             here[INSIDE + k] = strips[k]
         meanwhile()
         for copy in one_b:
             copy.wait_recv()
-        move(
-            send_a.at[1, step],
-            (32, NA, lambda a: my_b * NA + a),
-            cap_a,
-            my_a,
-            got_b[step],
-            me,
-            here,
-            NB * SLOTS,
+        two_a = send_in_plane(
+            1, step, 32, lambda a: my_b * NA + a, got_b[step], here, NB * SLOTS
         )
-        two_a = send_in_plane(1, step, here, NB * SLOTS)
+        keep(32, me, got_b[step], here, NB * SLOTS + my_a * SLOTS)
         for copy in one_a:
             copy.wait_recv()
-        move(
-            send_b.at[1, step],
-            (48, NB, lambda b: b * NA + my_a),
-            cap_b,
-            my_b,
-            got_a[step],
-            me,
-            here,
-            0,
-        )
-        two_b = send_along_y(1, step, here, 0)
+        two_b = send_along_y(1, step, 48, lambda b: b * NA + my_a, got_a[step], here, 0)
+        keep(48, me, got_a[step], here, my_b * SLOTS)
         for copy in two_b + two_a:
             copy.wait_recv()
         return one_a + one_b + two_a + two_b
 
-    def place_halos(step):
+    def add_halos(step, read, write):
         for t in range(TILES_DEV):
             for e in range(4):
                 i = 4 * t + e
@@ -298,12 +297,16 @@
                 for r in range(ROWS):
                     line = jnp.where(flipped, turned[7 - r : 8 - r], strip[r : r + 1])
                     if e < 2:
-                        side = side_w if e == 0 else side_e
+                        rows = slice(8 * r, 8 * r + 8)
+                        block = slice(0, 128) if e == 0 else slice(W - 128, W)
+                        edge = lane < TR if e == 0 else lane >= last
                         spread = lane_gather(jnp.broadcast_to(line, (8, 128)), TR * sub + member)
-                        side[t, 8 * r : 8 * r + 8, :] = spread
+                        more = jnp.where(edge, spread, 0.0)
                     else:
-                        at = 7 if e == 2 else 72
-                        field[step, t, at : at + 1, 128 * r : 128 * r + 128] = line
+                        rows = slice(0, 1) if e == 2 else slice(S - 1, S)
+                        block = slice(128 * r, 128 * r + 128)
+                        more = line
+                    write(t, rows, block, read(t, rows, block) + more * coef[1 + e, t, rows, block])
 
     def coefficients():
         at, to = iota((4 * S, W), 0), iota((4 * S, W), 1)
@@ -344,8 +347,8 @@
                 down = [pltpu.roll(cell, 128 - TR, axis=1) for cell in cells]
                 for b in range(BLOCKS):
                     block = slice(128 * b, 128 * b + 128)
-                    before = up[b - 1] if b > 0 else side_w[t, rows, :]
-                    after = down[b + 1] if b < BLOCKS - 1 else side_e[t, rows, :]
+                    before = up[b - 1] if b > 0 else 0.0
+                    after = down[b + 1] if b < BLOCKS - 1 else 0.0
                     west = jnp.where(lane < TR, before, up[b])
                     east = jnp.where(lane >= last, after, down[b])
                     south = field[step, t, top - 1 : top + 7, block]
@@ -357,11 +360,24 @@
                     )
                     write(t, rows, block, value)
 
+    def read_next(t, rows, block):
+        return field[1, t, rows.start + 8 : rows.stop + 8, block]
+
     def write_next(t, rows, block, value):
         field[1, t, rows.start + 8 : rows.stop + 8, block] = value
 
+    def read_out(t, rows, block):
+        return out_ref[t, rows, block]
+
     def write_out(t, rows, block, value):
         out_ref[t, rows, block] = value
+
+    def first_update():
+        coefficients()
+        advance(0, write_next)
+
+    def second_update():
+        advance(1, write_out)
 
     cut_strips(0)
     pl.semaphore_wait(barrier, len(everyone))
@@ -369,9 +385,11 @@
     for step in range(STEPS):
         if step > 0:
             cut_strips(step)
-        sent += exchange(step, coefficients if step == 0 else lambda: None)
-        place_halos(step)
-        advance(step, write_next if step == 0 else write_out)
+        sent += exchange(step, first_update if step == 0 else second_update)
+        if step == 0:
+            add_halos(step, read_next, write_next)
+        else:
+            add_halos(step, read_out, write_out)
 
     mine = level_sum.at[lev]
     for t in range(TILES_DEV):
@@ -430,8 +448,6 @@
         out_specs=(vmem, vmem),
         scratch_shapes=[
             pltpu.VMEM((2, TILES_DEV, S + 16, W), f32),
-            pltpu.VMEM((TILES_DEV, S, 128), f32),
-            pltpu.VMEM((TILES_DEV, S, 128), f32),
             pltpu.VMEM((5, TILES_DEV, S, W), f32),
             pltpu.VMEM((SLOTS, 8, 128), f32),
             pltpu.VMEM((2, 2, NA, SLOTS, 8, 128), f32),

time: 57.1 us -> 55.4 us (0.970)
  Pallas kernels: 53.2 us -> 51.5 us
    pallas_call x1, Pallas kernels: 51.3 us -> 48.2 us  [run_main(): pl.pallas_call(functools.partial(main_kernel, cap_a, cap_b), out_shape=(j...]
    pallas_call x1, Pallas kernels: 1.9 us -> 3.23 us  [body(): pl.pallas_call(plan_kernel, out_shape=(jax.ShapeDtypeStruct((80, 128), jn...]
where the time goes in v3:
time: 55.4 us; the launch traced here: 55.2 us
  Pallas kernels  51.5 us (93%)
  local copies, waits for them, and re-layouts  2.18 us (4%)
  between operations  1.32 us (2%)
    pallas_call x1, Pallas kernels, run_main(): pl.pallas_call(functools.partial(main_kernel, cap_a, cap_b), out_shape=(j...  48.2 us
    pallas_call x1, Pallas kernels, body(): pl.pallas_call(plan_kernel, out_shape=(jax.ShapeDtypeStruct((80, 128), jn...  3.23 us
    unnamed x8, local copies, waits for them, and re-layouts  2.18 us

profile of v3, /device:TPU:1, one launch (start us, length us, event | category | flops | bytes accessed | tf_op | source)
XLA Modules:
  0.0 55.2 jit_solution(873978579775832624)
XLA Ops:
  0.6 3.2 %plan.1 = (s32[80,128]{1,0:T(8,128)S(1)}, f32[1,1]{1,0:T(1,128)}) custom-call(s32[4,384]{1,0:T(4,128)} %bitcast.28, s32[4,384]{1,0:T(4,128)} %bitcast.29), custom_call_target="tpu_custom_call" | custom-call | tf_op jit(solution)/shard_map/plan/pallas_call | solution.py:488
  4.5 0.0 copy-start.2
  4.5 0.0 copy-start
  4.5 0.0 copy-start.1
  4.6 0.6 %copy-done.2 = s32[3]{0:T(128)S(1)} copy-done((s32[3]{0:T(128)S(1)}, s32[3]{0:T(128)}, u32[]{:S(2)}) %copy-start.2) | copy-done | bytes 36
  5.2 0.0 copy-done
  5.2 0.0 copy-done.1
  5.2 48.4 %conditional.1 = (f32[3,16,128]{2,1,0:T(8,128)S(1)}, f32[3,1,64,1024]{3,2,1,0:T(8,128)S(1)}) conditional(s32[]{:T(128)} %bitcast.16, (f32[3,1,64,1024]{3,2,1,0:T(8,128)}, f32[3,1,64,65]{3,2,1,0:T(8,128)}, s32[80,128]{1,0:T(8,128)S(1)}, s32[3]{0:T(128)S(1)}, f32[3,64,65]{2,1,0:T(8,128)}, /*index=5*/f32[3,64,64]{2,1,0:T(8,128)}, ...), branch_computations={%region_0.0_spmd, %region_1.0_spmd} | conditional | bytes 16 | solution.py:508
  5.2 48.2 %transport_2_4.1 = (f32[3,64,1024]{2,1,0:T(8,128)S(1)}, f32[3,16,128]{2,1,0:T(8,128)S(1)}) custom-call(s32[80,128]{1,0:T(8,128)S(1)} %get-tuple-element.41.plan_ref, s32[3]{0:T(128)S(1)} %get-tuple-element.42.count_ref, f32[3,64,1024]{2,1,0:T(8,128)} %bitcast.20, f32[3,64,65]{2,1,0:T(8,128)} %bitcast.24, f32[3,64,65]{2,1,0:T(8,128)} %get-tuple-element.45.cy_ref, ...), custom_call_target="tpu_custom_call" | custom-call | tf_op jit(solution)/shard_map/cond/branch_0_fun/transport_2_4/pallas_call | solution.py:441
  53.7 0.9 %copy.24 = f32[3,1,64,1024]{3,2,1,0:T(8,128)} copy(f32[3,1,64,1024]{3,2,1,0:T(8,128)S(1)} %get-tuple-element.96) | data formatting | bytes 1572864
  54.6 0.6 %copy.25 = f32[3,16,128]{2,1,0:T(8,128)} copy(f32[3,16,128]{2,1,0:T(8,128)S(1)} %get-tuple-element.97) | data formatting | bytes 49152
Async XLA Ops:
  4.5 0.7 %copy-start.2 = (s32[3]{0:T(128)S(1)}, s32[3]{0:T(128)}, u32[]{:S(2)}) copy-start(s32[3]{0:T(128)} %param.19) | copy-start | bytes 40
  4.5 0.7 %copy-start = (s32[3,128]{1,0:T(4,128)S(1)}, s32[3,128]{1,0:T(4,128)}, u32[]{:S(2)}) copy-start(s32[3,128]{1,0:T(4,128)} %param.18) | copy-start | bytes 4612
  4.5 0.7 %copy-start.1 = (f32[3,1,128]{2,1,0:T(1,128)S(1)}, f32[3,1,128]{2,1,0:T(1,128)}, u32[]{:S(2)}) copy-start(f32[3,1,128]{2,1,0:T(1,128)} %param.17) | copy-start | bytes 4612
